TPU v7x, 32 devices: a whole 2x2x4 slice. The times are simulated.
32 devices in a mesh: groups: 2 (over y), box: 4 (over z), dir: 2 (over x), sub: 2 (over core).
Axes of the slice: x: 2, y: 2, z: 4, core: 2. Of those that a mesh axis runs over, the one named last changes fastest.
Arguments:
- history_currents: bfloat16 [128, 16, 128], P(('groups', 'box')), parts along dimension 0, may hold values from -6 to 6
- history_rays: bfloat16 [128, 16, 10240], P(('groups', 'box'), None, ('dir', 'sub')), parts along dimension 0, may hold values from -6 to 6
- incident: float32 [128, 4, 128], P(('groups', 'box')), parts along dimension 0, may hold values from -6 to 6
- near_blocks: bfloat16 [64, 12, 4, 128, 128], P('box', None, ('dir', 'sub')), may hold values from -0.0546875 to 0.0546875
- near_partners: int32 [64, 12], P('box'), may hold values from 0 to 63, as said below
- self_inverse: float32 [64, 128, 128], P('box'), may hold values from -0.5 to 0.5
- projection: bfloat16 [128, 10240], P(None, ('dir', 'sub')), may hold values from -0.5 to 0.5
- reception: bfloat16 [10240, 128], P(('dir', 'sub')), may hold values from -0.03125 to 0.03125
- translations: bfloat16 [316, 10240], P(None, ('dir', 'sub')), may hold values from -6 to 6
- send_source: int32 [4, 4, 8], P('box'), may hold values from 0 to 15
- send_delay: int32 [4, 4, 8], P('box'), may hold values from 1 to 16
- send_target: int32 [4, 4, 8], P('box'), may hold values from 0 to 15
- send_class: int32 [4, 4, 8], P('box'), may hold values from 0 to 315
- slot_counts: int32 [4, 4], P('box'), may hold values from 0 to 8, as said below
Outputs:
- currents: bfloat16 [128, 4, 128], P(('groups', 'box')), parts along dimension 0
- rays: bfloat16 [128, 4, 10240], P(('groups', 'box'), None, ('dir', 'sub')), parts along dimension 0
There are 2 independent parts, one for each index of `groups`. A program takes and returns all parts, laid end to end along the dimension named above; an argument that names none is the same for every part. Nothing has to cross between parts.
Inputs may be any that keep to these rules, and one draw needn't show every extreme that they name: |near_partners[b, n] - b| <= 16; near_partners[b, 0] = b. `slot_counts`: every sender has 8 live slots to some receiver, and some receiver has 8 live slots from every sender.
All inputs are finite; a program needn't handle non-finite values.
Results may differ from a plain program's by a relative error of at most 0.0054.
Values may be sent and summed in bfloat16 or wider, within the bound.
A program may use at most 64 MiB of HBM per device.

v0:
```python
import jax
import jax.numpy as jnp
from jax import lax
from jax.sharding import PartitionSpec as P


def padded(value, sides, width):
    for axis, dim in sides:
        size, length = (lax.axis_size(axis), value.shape[dim])
        up = [(i, (i + 1) % size) for i in range(size - 1)]
        down = [(j, i) for i, j in up]
        last = lax.slice_in_dim(value, length - width, length, axis=dim)
        leading = lax.slice_in_dim(value, 0, width, axis=dim)
        before = lax.ppermute(last, axis, up)
        after = lax.ppermute(leading, axis, down)
        value = jnp.concatenate([before, value, after], axis=dim)
    return value


def body(
    history_currents,
    history_rays,
    incident,
    near_blocks,
    near_partners,
    self_inverse,
    projection,
    reception,
    translations,
    send_source,
    send_delay,
    send_target,
    send_class,
    slot_counts,
):
    box_count = history_currents.shape[0]
    hist_len = history_currents.shape[1]
    size_s = history_currents.shape[2]
    ray_width = history_rays.shape[2]
    step_count = incident.shape[1]
    lag_count = near_blocks.shape[2]
    peer_count = lax.axis_size("box")
    box_index = lax.axis_index("box")
    lag_part = lax.axis_index(("dir", "sub"))
    lag_span = lag_count * lax.axis_size(("dir", "sub"))
    buffer_len = hist_len + step_count
    source_box = send_source[0]
    delay_ids = send_delay[0]
    target_box = send_target[0]
    class_ids = send_class[0]
    capacity = source_box.shape[1]
    live_slots = jnp.arange(capacity)[None, :] < slot_counts[0][:, None]
    local_partner = near_partners - (box_index - 1) * box_count
    cur_buf = jnp.concatenate(
        [history_currents, jnp.zeros((box_count, step_count, size_s), jnp.bfloat16)], axis=1
    )
    ray_buf = jnp.concatenate(
        [history_rays, jnp.zeros((box_count, step_count, ray_width), jnp.bfloat16)], axis=1
    )
    send_factors = jnp.take(translations, class_ids.reshape(-1), axis=0).astype(jnp.float32)
    dest_rows = (jnp.arange(peer_count)[:, None] * box_count + target_box).reshape(-1)
    for moment in range(step_count):
        ray_table = ray_buf.reshape(box_count * buffer_len, ray_width)
        row_ids = (source_box * buffer_len + hist_len + moment - delay_ids).reshape(-1)
        outgoing = jnp.take(ray_table, row_ids, axis=0).reshape(peer_count, capacity, ray_width)
        slot_terms = outgoing.reshape(-1, ray_width).astype(jnp.float32) * send_factors
        slot_terms = jnp.where(live_slots.reshape(-1)[:, None], slot_terms, jnp.float32(0.0))
        match = (
            dest_rows[None, :] == jnp.arange(lax.axis_size("box") * box_count)[:, None]
        ).astype(jnp.float32)
        incoming = lax.psum_scatter(
            jnp.dot(
                match,
                slot_terms,
                precision=lax.Precision.HIGHEST,
                preferred_element_type=jnp.float32,
            ),
            "box",
            scatter_dimension=0,
            tiled=True,
        )
        window = padded(
            cur_buf[:, hist_len + moment - lag_span : hist_len + moment], (("box", 0),), box_count
        )
        own_lags = lax.dynamic_slice_in_dim(
            window, lag_span - (lag_part + 1) * lag_count, lag_count, 1
        )[:, ::-1]
        partner_hist = jnp.take(own_lags, local_partner, axis=0)
        near_field = jnp.einsum(
            "bnlst,bnlt->bs", near_blocks, partner_hist, preferred_element_type=jnp.float32
        )
        far_field = jnp.dot(
            incoming.astype(jnp.bfloat16), reception, preferred_element_type=jnp.float32
        )
        total_field = lax.psum(near_field + far_field, ("dir", "sub"))
        current = jnp.einsum(
            "bst,bt->bs",
            self_inverse,
            incident[:, moment] - total_field,
            precision=lax.Precision.HIGHEST,
        )
        current_low = current.astype(jnp.bfloat16)
        new_rays = jnp.dot(current_low, projection, preferred_element_type=jnp.float32).astype(
            jnp.bfloat16
        )
        cur_buf = cur_buf.at[:, hist_len + moment].set(current_low)
        ray_buf = ray_buf.at[:, hist_len + moment].set(new_rays)
    return (cur_buf[:, hist_len:], ray_buf[:, hist_len:])


def solution(mesh):
    return jax.shard_map(
        body,
        mesh=mesh,
        in_specs=(
            P(("groups", "box"), None, None),
            P(("groups", "box"), None, ("dir", "sub")),
            P(("groups", "box"), None, None),
            P("box", None, ("dir", "sub"), None, None),
            P("box", None),
            P("box", None, None),
            P(None, ("dir", "sub")),
            P(("dir", "sub"), None),
            P(None, ("dir", "sub")),
            P("box", None, None),
            P("box", None, None),
            P("box", None, None),
            P("box", None, None),
            P("box", None),
        ),
        out_specs=(P(("groups", "box"), None, None), P(("groups", "box"), None, ("dir", "sub"))),
        check_vma=False,
    )
```

profile of v0, /device:TPU:0, one launch (start us, length us, event | category | flops | bytes accessed | tf_op | source)
XLA Modules:
  0.0 214.1 jit_solution(3319357043621507810)
XLA Ops:
  8.2 4.9 %collective-permute-start = (bf16[16,4,128]{2,0,1:T(8,128)(2,1)S(1)}, bf16[16,4,128]{2,0,1:T(8,128)(2,1)S(1)}, u32[]{:S(2)}, u32[]{:S(2)}) collective-permute-start(bf16[16,4,128]{2,0,1:T(8,128)(2,1)S(1)} %slice.218), channel_id=1, source_target_pairs={{0,4},{4,8},{8,12},{1,5},{5,9},{9,13},{2,6},{6,10},{10,14},{3,7},{... | collective-permute-start | bytes 49160 | tf_op jit(solution)/shard_map/ppermute | solution.py:14
  13.1 1.3 collective-permute-start.1
  17.4 2.7 %concatenate.36 = bf16[16,20,2560]{2,1,0:T(8,128)(2,1)} pad(bf16[16,16,2560]{2,1,0:T(8,128)(2,1)} %param.35, bf16[]{:T(256)} %constant.247.clone.1), padding=0_0x0_4x0_0 | pad | bytes 2949122 | tf_op jit(solution)/shard_map/concatenate | solution.py:57
  20.2 3.5 %reshape.380 = bf16[320,2560]{1,0:T(8,128)(2,1)} reshape(bf16[16,20,2560]{2,1,0:T(8,128)(2,1)} %concatenate.36) | data formatting | bytes 3276800 | tf_op jit(solution)/shard_map/reshape | solution.py:63
  24.2 2.5 %gather_fusion.2 = bf16[32,2560]{1,0:T(8,128)(2,1)S(1)} fusion(bf16[320,2560]{1,0:T(8,128)(2,1)} %reshape.380, s32[1024]{0:T(1024)S(1)} %pad_clamp_fusion.4), kind=kCustom, calls=%fused_computation.1.clone | custom fusion | bytes 327808 | tf_op jit(solution)/shard_map/jit(_take)/gather | solution.py:65
  27.3 1.4 fusion.13
  32.5 4.6 %fusion.6 = f32[16,1,128,1]{2,1,3,0:T(1,128)S(1)} fusion(bf16[16,12,1,128,128]{4,3,2,1,0:T(8,128)(2,1)} %param.37, bf16[16,12,128,1]{2,1,0,3:T(8,128)(2,1)S(1)} %select_bitcast_fusion.3), kind=kOutput, calls=%fused_computation.15 | convolution fusion | flops 6291456 | bytes 6348800 | tf_op jit(solution)/shard_map/bnlst,bnlt->bs/dot_general | solution.py:89
  37.2 16.2 %reduce-scatter.5.cloned.1.call-done = f32[16,2560]{1,0:T(8,128)} async-done(((f32[64,2560]{1,0:T(8,128)}), f32[16,2560]{1,0:T(8,128)}) %reduce-scatter.5.cloned.1.call-update) | async-done | bytes 163856 | tf_op jit(solution)/shard_map/reduce_scatter | solution.py:71
  54.5 5.8 %psum.28 = f32[16,128]{1,0:T(8,128)S(1)} all-reduce(f32[16,128]{1,0:T(8,128)S(1)} %convolution_add_fusion.3), channel_id=1, replica_groups=mesh['groups'=2,'box'=4,'dir'=2,'sub'=2] {'dir','sub'}, use_global_device_ids=true, to_apply=%region_1.0 | all-reduce | flops 2048 | bytes 16384 | tf_op jit(solution)/shard_map/psum | solution.py:95
  60.9 1.7 fusion.86
  62.7 1.3 fusion.8
  64.8 3.5 %scatter.29 = bf16[16,20,2560]{2,1,0:T(8,128)(2,1)} dynamic-update-slice(bf16[16,20,2560]{2,1,0:T(8,128)(2,1)} %concatenate.36, bf16[16,1,2560]{2,1,0:T(2,128)(2,1)} %copy.22, s32[]{:T(128)} %constant.248.clone.1, s32[]{:T(128)} %constant.257.clone.1, s32[]{:T(128)} %constant.248.clone.1) | dynamic-update-slice | bytes 163844 | tf_op jit(solution)/shard_map/scatter | solution.py:107
  68.3 3.5 %reshape.384 = bf16[320,2560]{1,0:T(8,128)(2,1)} reshape(bf16[16,20,2560]{2,1,0:T(8,128)(2,1)} %scatter.29) | data formatting | bytes 3276800 | tf_op jit(solution)/shard_map/reshape | solution.py:63
  71.8 3.2 %gather_fusion.4 = bf16[32,2560]{1,0:T(8,128)(2,1)} fusion(bf16[320,2560]{1,0:T(8,128)(2,1)} %reshape.384, s32[1024]{0:T(1024)} %pad_clamp_fusion.2), kind=kCustom, calls=%fused_computation.5.clone | custom fusion | bytes 327808 | tf_op jit(solution)/shard_map/jit(_take)/gather | solution.py:65
  75.1 2.3 %fusion.16 = f32[64,2560]{1,0:T(8,128)} fusion(bf16[32,2560]{1,0:T(8,128)(2,1)} %gather_fusion.4, pred[32]{0:T(512)(128)(4,1)} %get-tuple-element.118, pred[32]{0:T(512)(128)(4,1)S(1)} %lt.66, s32[32]{0:T(128)S(1)} %copy-done.8, bf16[32,2560]{1,0:T(8,128)(2,1)S(1)} %gather_fusion, pred[32]{0:T(512)(128)(4,1)S(1)} %compare_and_fusion.5), kind=kOutput, calls=%fused_computation.36 | convolution fusion | flops 63408128 | bytes 983264 | tf_op jit(solution)/shard_map/dot_general | solution.py:72
  81.3 1.3 collective-permute-start.3
  83.8 3.5 %collective-permute-done.3 = bf16[16,4,128]{2,0,1:T(8,128)(2,1)S(1)} collective-permute-done((bf16[16,4,128]{2,0,1:T(8,128)(2,1)S(1)}, bf16[16,4,128]{2,0,1:T(8,128)(2,1)S(1)}, u32[]{:S(2)}, u32[]{:S(2)}) %collective-permute-start.3) | collective-permute-done | bytes 16416 | tf_op jit(solution)/shard_map/ppermute | solution.py:15
  87.3 1.4 gather_fusion.3
  88.7 1.4 reshape.502
  91.1 4.6 %fusion.4 = f32[16,1,128,1]{2,1,3,0:T(1,128)S(1)} fusion(bf16[16,12,1,128,128]{4,3,2,1,0:T(8,128)(2,1)} %param.37, bf16[16,12,128,1]{2,1,0,3:T(8,128)(2,1)S(1)} %select_bitcast_fusion.2), kind=kOutput, calls=%fused_computation.13 | convolution fusion | flops 6291456 | bytes 6348800 | tf_op jit(solution)/shard_map/bnlst,bnlt->bs/dot_general | solution.py:89
  95.7 3.6 %reduce-scatter.7.cloned.1.call-done = f32[16,2560]{1,0:T(8,128)} async-done(((f32[64,2560]{1,0:T(8,128)}), f32[16,2560]{1,0:T(8,128)}) %reduce-scatter.7.cloned.1.call-update) | async-done | bytes 163856 | tf_op jit(solution)/shard_map/reduce_scatter | solution.py:71
  100.4 5.8 %psum.29 = f32[16,128]{1,0:T(8,128)S(1)} all-reduce(f32[16,128]{1,0:T(8,128)S(1)} %convolution_add_fusion.2), channel_id=1, replica_groups=mesh['groups'=2,'box'=4,'dir'=2,'sub'=2] {'dir','sub'}, use_global_device_ids=true, to_apply=%region_3.6 | all-reduce | flops 2048 | bytes 16384 | tf_op jit(solution)/shard_map/psum | solution.py:95
  106.9 1.7 fusion.87
  110.7 3.5 %scatter.31 = bf16[16,20,2560]{2,1,0:T(8,128)(2,1)} dynamic-update-slice(bf16[16,20,2560]{2,1,0:T(8,128)(2,1)} %scatter.29, bf16[16,1,2560]{2,1,0:T(2,128)(2,1)} %copy.23, s32[]{:T(128)} %constant.248.clone.1, s32[]{:T(128)} %constant.263.clone.1, s32[]{:T(128)} %constant.248.clone.1) | dynamic-update-slice | bytes 163844 | tf_op jit(solution)/shard_map/scatter | solution.py:107
  114.3 3.5 %reshape.388 = bf16[320,2560]{1,0:T(8,128)(2,1)} reshape(bf16[16,20,2560]{2,1,0:T(8,128)(2,1)} %scatter.31) | data formatting | bytes 3276800 | tf_op jit(solution)/shard_map/reshape | solution.py:63
  117.8 3.2 %gather_fusion.6 = bf16[32,2560]{1,0:T(8,128)(2,1)} fusion(bf16[320,2560]{1,0:T(8,128)(2,1)} %reshape.388, s32[1024]{0:T(1024)} %pad_clamp_fusion.1), kind=kCustom, calls=%fused_computation.6.clone | custom fusion | bytes 327808 | tf_op jit(solution)/shard_map/jit(_take)/gather | solution.py:65
  121.0 2.3 %fusion.19 = f32[64,2560]{1,0:T(8,128)} fusion(bf16[32,2560]{1,0:T(8,128)(2,1)} %gather_fusion.6, pred[32]{0:T(512)(128)(4,1)S(1)} %copy-done.16, pred[32]{0:T(512)(128)(4,1)S(1)} %copy-done.5, s32[32]{0:T(128)S(1)} %copy-done.9, bf16[32,2560]{1,0:T(8,128)(2,1)S(1)} %gather_fusion, pred[32]{0:T(512)(128)(4,1)S(1)} %compare_and_fusion.5), kind=kOutput, calls=%fused_computation.38 | convolution fusion | flops 63408128 | bytes 983264 | tf_op jit(solution)/shard_map/dot_general | solution.py:72
  126.0 1.5 collective-permute-start.5
  128.7 2.9 %collective-permute-done.5 = bf16[16,4,128]{2,0,1:T(8,128)(2,1)S(1)} collective-permute-done((bf16[16,4,128]{2,0,1:T(8,128)(2,1)S(1)}, bf16[16,4,128]{2,0,1:T(8,128)(2,1)S(1)}, u32[]{:S(2)}, u32[]{:S(2)}) %collective-permute-start.5) | collective-permute-done | bytes 16416 | tf_op jit(solution)/shard_map/ppermute | solution.py:15
  131.6 1.4 gather_fusion.5
  133.0 1.4 reshape.509
  135.4 4.6 %fusion.2 = f32[16,1,128,1]{2,1,3,0:T(1,128)S(1)} fusion(bf16[16,12,1,128,128]{4,3,2,1,0:T(8,128)(2,1)} %param.37, bf16[16,12,128,1]{2,1,0,3:T(8,128)(2,1)S(1)} %select_bitcast_fusion.1), kind=kOutput, calls=%fused_computation.11 | convolution fusion | flops 6291456 | bytes 6348800 | tf_op jit(solution)/shard_map/bnlst,bnlt->bs/dot_general | solution.py:89
  140.0 5.0 %reduce-scatter.9.cloned.1.call-done = f32[16,2560]{1,0:T(8,128)} async-done(((f32[64,2560]{1,0:T(8,128)}), f32[16,2560]{1,0:T(8,128)}) %reduce-scatter.9.cloned.1.call-update) | async-done | bytes 163856 | tf_op jit(solution)/shard_map/reduce_scatter | solution.py:71
  146.1 5.8 %psum.30 = f32[16,128]{1,0:T(8,128)S(1)} all-reduce(f32[16,128]{1,0:T(8,128)S(1)} %convolution_add_fusion.1), channel_id=1, replica_groups=mesh['groups'=2,'box'=4,'dir'=2,'sub'=2] {'dir','sub'}, use_global_device_ids=true, to_apply=%region_5.8 | all-reduce | flops 2048 | bytes 16384 | tf_op jit(solution)/shard_map/psum | solution.py:95
  151.9 1.7 fusion.88
  155.8 3.5 %scatter.35 = bf16[16,20,2560]{2,1,0:T(8,128)(2,1)} dynamic-update-slice(bf16[16,20,2560]{2,1,0:T(8,128)(2,1)} %scatter.31, bf16[16,1,2560]{2,1,0:T(2,128)(2,1)} %copy.24, s32[]{:T(128)} %constant.248.clone.1, s32[]{:T(128)} %constant.264.clone.1, s32[]{:T(128)} %constant.248.clone.1) | dynamic-update-slice | bytes 163844 | tf_op jit(solution)/shard_map/scatter | solution.py:107
  159.3 3.5 %reshape.392 = bf16[320,2560]{1,0:T(8,128)(2,1)} reshape(bf16[16,20,2560]{2,1,0:T(8,128)(2,1)} %scatter.35) | data formatting | bytes 3276800 | tf_op jit(solution)/shard_map/reshape | solution.py:63
  162.8 3.2 %gather_fusion.8 = bf16[32,2560]{1,0:T(8,128)(2,1)} fusion(bf16[320,2560]{1,0:T(8,128)(2,1)} %reshape.392, s32[1024]{0:T(1024)} %pad_clamp_fusion), kind=kCustom, calls=%fused_computation.7.clone | custom fusion | bytes 327808 | tf_op jit(solution)/shard_map/jit(_take)/gather | solution.py:65
  166.1 2.3 %fusion.22 = f32[64,2560]{1,0:T(8,128)} fusion(bf16[32,2560]{1,0:T(8,128)(2,1)} %gather_fusion.8, pred[32]{0:T(512)(128)(4,1)S(1)} %copy-done.15, pred[32]{0:T(512)(128)(4,1)S(1)} %copy-done.6, s32[32]{0:T(128)S(1)} %copy-done.10, bf16[32,2560]{1,0:T(8,128)(2,1)S(1)} %gather_fusion, pred[32]{0:T(512)(128)(4,1)S(1)} %compare_and_fusion.5), kind=kOutput, calls=%fused_computation.40 | convolution fusion | flops 63408128 | bytes 983264 | tf_op jit(solution)/shard_map/dot_general | solution.py:72
  171.0 1.3 collective-permute-start.7
  172.4 4.2 %collective-permute-done.7 = bf16[16,4,128]{2,0,1:T(8,128)(2,1)S(1)} collective-permute-done((bf16[16,4,128]{2,0,1:T(8,128)(2,1)S(1)}, bf16[16,4,128]{2,0,1:T(8,128)(2,1)S(1)}, u32[]{:S(2)}, u32[]{:S(2)}) %collective-permute-start.7) | collective-permute-done | bytes 16416 | tf_op jit(solution)/shard_map/ppermute | solution.py:15
  177.6 4.6 %fusion = f32[16,1,128,1]{2,1,3,0:T(1,128)S(1)} fusion(bf16[16,12,1,128,128]{4,3,2,1,0:T(8,128)(2,1)} %param.37, bf16[16,12,128,1]{2,1,0,3:T(8,128)(2,1)S(1)} %select_bitcast_fusion), kind=kOutput, calls=%fused_computation.9 | convolution fusion | flops 6291456 | bytes 6348800 | tf_op jit(solution)/shard_map/bnlst,bnlt->bs/dot_general | solution.py:89
  182.1 8.0 %reduce-scatter.11.cloned.1.call-done = f32[16,2560]{1,0:T(8,128)} async-done(((f32[64,2560]{1,0:T(8,128)}), f32[16,2560]{1,0:T(8,128)}) %reduce-scatter.11.cloned.1.call-update) | async-done | bytes 163856 | tf_op jit(solution)/shard_map/reduce_scatter | solution.py:71
  191.3 5.8 %psum.31 = f32[16,128]{1,0:T(8,128)S(1)} all-reduce(f32[16,128]{1,0:T(8,128)S(1)} %convolution_add_fusion), channel_id=1, replica_groups=mesh['groups'=2,'box'=4,'dir'=2,'sub'=2] {'dir','sub'}, use_global_device_ids=true, to_apply=%region_7.10 | all-reduce | flops 2048 | bytes 16384 | tf_op jit(solution)/shard_map/psum | solution.py:95
  197.0 1.7 fusion.89
  198.8 1.3 fusion.11
  200.8 3.5 %scatter.39 = bf16[16,20,2560]{2,1,0:T(8,128)(2,1)} dynamic-update-slice(bf16[16,20,2560]{2,1,0:T(8,128)(2,1)} %scatter.35, bf16[16,1,2560]{2,1,0:T(2,128)(2,1)S(1)} %copy.25, s32[]{:T(128)} %constant.248.clone.1, s32[]{:T(128)} %constant.265.clone.1, s32[]{:T(128)} %constant.248.clone.1) | dynamic-update-slice | bytes 163844 | tf_op jit(solution)/shard_map/scatter | solution.py:107
  204.3 1.9 slice.223
  (122 shorter events, 36.3 us)
Async XLA Ops:
  7.2 19.5 %copy-start = (bf16[316,2560]{1,0:T(8,128)(2,1)S(1)}, bf16[316,2560]{1,0:T(8,128)(2,1)}, u32[]{:S(2)}) copy-start(bf16[316,2560]{1,0:T(8,128)(2,1)} %param.42) | copy-start | bytes 4853764
  7.2 46.2 %reduce-scatter.5.cloned.1.call-start = ((), (), s32[]{:S(2)}) async-start(), calls=%async_computation.4 | async-start | bytes 819200 | tf_op jit(solution)/shard_map/reduce_scatter | solution.py:71
  8.2 23.4 %collective-permute-start = (bf16[16,4,128]{2,0,1:T(8,128)(2,1)S(1)}, bf16[16,4,128]{2,0,1:T(8,128)(2,1)S(1)}, u32[]{:S(2)}, u32[]{:S(2)}) collective-permute-start(bf16[16,4,128]{2,0,1:T(8,128)(2,1)S(1)} %slice.218), channel_id=1, source_target_pairs={{0,4},{4,8},{8,12},{1,5},{5,9},{9,13},{2,6},{6,10},{10,14},{3,7},{... | collective-permute-start | bytes 49160 | tf_op jit(solution)/shard_map/ppermute | solution.py:14
  13.1 18.4 %collective-permute-start.1 = (bf16[16,4,128]{2,0,1:T(8,128)(2,1)S(1)}, bf16[16,4,128]{2,0,1:T(8,128)(2,1)S(1)}, u32[]{:S(2)}, u32[]{:S(2)}) collective-permute-start(bf16[16,4,128]{2,0,1:T(8,128)(2,1)S(1)} %slice.218), channel_id=1, source_target_pairs={{4,0},{8,4},{12,8},{5,1},{9,5},{13,9},{6,2},{10,6},{14,10},{7,3},{... | collective-permute-start | bytes 49160 | tf_op jit(solution)/shard_map/ppermute | solution.py:15
  20.2 3.7 %copy-start.17 = (s32[1,4,8]{2,1,0:T(4,128)S(1)}, s32[1,4,8]{2,1,0:T(4,128)}, u32[]{:S(2)}) copy-start(s32[1,4,8]{2,1,0:T(4,128)} %param.45) | copy-start | bytes 388
  20.2 3.8 %copy-start.18 = (s32[1,4]{1,0:T(1,128)S(1)}, s32[1,4]{1,0:T(1,128)}, u32[]{:S(2)}) copy-start(s32[1,4]{1,0:T(1,128)} %param.47) | copy-start | bytes 52
  24.2 50.9 %copy-start.4 = (pred[32]{0:T(512)(128)(4,1)}, pred[32]{0:T(512)(128)(4,1)S(1)}, u32[]{:S(2)}) copy-start(pred[32]{0:T(512)(128)(4,1)S(1)} %lt.66) | copy-start | bytes 100
  24.2 4.6 %copy-start.11 = (s32[16,12]{1,0:T(8,128)S(1)}, s32[16,12]{1,0:T(8,128)}, u32[]{:S(2)}) copy-start(s32[16,12]{1,0:T(8,128)} %param.38) | copy-start | bytes 2308
  24.2 5.5 %copy-start.3 = (f32[16,4,128]{2,1,0:T(4,128)S(1)}, f32[16,4,128]{2,1,0:T(4,128)}, u32[]{:S(2)}) copy-start(f32[16,4,128]{2,1,0:T(4,128)} %param.36) | copy-start | bytes 98308
  27.3 1.5 copy-start.7
  28.7 70.6 %reduce-scatter.7.cloned.1.call-start = ((), (), s32[]{:S(2)}) async-start(), calls=%async_computation.5 | async-start | bytes 819200 | tf_op jit(solution)/shard_map/reduce_scatter | solution.py:71
  29.0 8.1 %copy-start.12 = (s32[32]{0:T(128)}, s32[32]{0:T(128)S(1)}, u32[]{:S(2)}) copy-start(s32[32]{0:T(128)S(1)} %sub.66) | copy-start | bytes 388
  29.1 8.1 %copy-start.14 = (s32[32]{0:T(128)}, s32[32]{0:T(128)S(1)}, u32[]{:S(2)}) copy-start(s32[32]{0:T(128)S(1)} %sub.69) | copy-start | bytes 388
  32.5 20.9 %copy-start.2 = (bf16[2560,128]{1,0:T(8,128)(2,1)S(1)}, bf16[2560,128]{1,0:T(8,128)(2,1)}, u32[]{:S(2)}) copy-start(bf16[2560,128]{1,0:T(8,128)(2,1)} %param.41) | copy-start | bytes 1966084
  32.5 28.4 %copy-start.1 = (f32[16,128,128]{2,1,0:T(8,128)S(1)}, f32[16,128,128]{2,1,0:T(8,128)}, u32[]{:S(2)}) copy-start(f32[16,128,128]{2,1,0:T(8,128)} %param.39) | copy-start | bytes 3145732
  68.3 6.8 %copy-start.8 = (s32[32]{0:T(128)S(1)}, s32[32]{0:T(128)}, u32[]{:S(2)}) copy-start(s32[32]{0:T(128)} %copy-done.7) | copy-start | bytes 388
  71.8 5.6 %copy-start.13 = (s32[32]{0:T(128)S(1)}, s32[32]{0:T(128)}, u32[]{:S(2)}) copy-start(s32[32]{0:T(128)} %copy-done.12) | copy-start | bytes 388
  77.4 67.6 %reduce-scatter.9.cloned.1.call-start = ((), (), s32[]{:S(2)}) async-start(), calls=%async_computation.6 | async-start | bytes 819200 | tf_op jit(solution)/shard_map/reduce_scatter | solution.py:71
  80.0 3.9 %collective-permute-start.2 = (bf16[16,4,128]{2,0,1:T(8,128)(2,1)S(1)}, bf16[16,4,128]{2,0,1:T(8,128)(2,1)S(1)}, u32[]{:S(2)}, u32[]{:S(2)}) collective-permute-start(bf16[16,4,128]{2,0,1:T(8,128)(2,1)S(1)} %slice.219), channel_id=1, source_target_pairs={{0,4},{4,8},{8,12},{1,5},{5,9},{9,13},{2,6},{6,10},{10,14},{3,7},{... | collective-permute-start | bytes 49160 | tf_op jit(solution)/shard_map/ppermute | solution.py:14
  81.3 6.1 %collective-permute-start.3 = (bf16[16,4,128]{2,0,1:T(8,128)(2,1)S(1)}, bf16[16,4,128]{2,0,1:T(8,128)(2,1)S(1)}, u32[]{:S(2)}, u32[]{:S(2)}) collective-permute-start(bf16[16,4,128]{2,0,1:T(8,128)(2,1)S(1)} %slice.219), channel_id=1, source_target_pairs={{4,0},{8,4},{12,8},{5,1},{9,5},{13,9},{6,2},{10,6},{14,10},{7,3},{... | collective-permute-start | bytes 49160 | tf_op jit(solution)/shard_map/ppermute | solution.py:15
  114.2 6.8 %copy-start.5 = (pred[32]{0:T(512)(128)(4,1)S(1)}, pred[32]{0:T(512)(128)(4,1)}, u32[]{:S(2)}) copy-start(pred[32]{0:T(512)(128)(4,1)} %copy-done.4) | copy-start | bytes 100
  114.3 6.8 %copy-start.9 = (s32[32]{0:T(128)S(1)}, s32[32]{0:T(128)}, u32[]{:S(2)}) copy-start(s32[32]{0:T(128)} %copy-done.7) | copy-start | bytes 388
  114.3 6.8 %copy-start.16 = (pred[32]{0:T(512)(128)(4,1)S(1)}, pred[32]{0:T(512)(128)(4,1)}, u32[]{:S(2)}) copy-start(pred[32]{0:T(512)(128)(4,1)} %get-tuple-element.117) | copy-start | bytes 100
  123.4 66.8 %reduce-scatter.11.cloned.1.call-start = ((), (), s32[]{:S(2)}) async-start(), calls=%async_computation.7 | async-start | bytes 819200 | tf_op jit(solution)/shard_map/reduce_scatter | solution.py:71
  124.7 4.0 %collective-permute-start.4 = (bf16[16,4,128]{2,0,1:T(8,128)(2,1)S(1)}, bf16[16,4,128]{2,0,1:T(8,128)(2,1)S(1)}, u32[]{:S(2)}, u32[]{:S(2)}) collective-permute-start(bf16[16,4,128]{2,0,1:T(8,128)(2,1)S(1)} %slice.220), channel_id=1, source_target_pairs={{0,4},{4,8},{8,12},{1,5},{5,9},{9,13},{2,6},{6,10},{10,14},{3,7},{... | collective-permute-start | bytes 49160 | tf_op jit(solution)/shard_map/ppermute | solution.py:14
  126.0 5.6 %collective-permute-start.5 = (bf16[16,4,128]{2,0,1:T(8,128)(2,1)S(1)}, bf16[16,4,128]{2,0,1:T(8,128)(2,1)S(1)}, u32[]{:S(2)}, u32[]{:S(2)}) collective-permute-start(bf16[16,4,128]{2,0,1:T(8,128)(2,1)S(1)} %slice.220), channel_id=1, source_target_pairs={{4,0},{8,4},{12,8},{5,1},{9,5},{13,9},{6,2},{10,6},{14,10},{7,3},{... | collective-permute-start | bytes 49160 | tf_op jit(solution)/shard_map/ppermute | solution.py:15
  159.3 6.8 %copy-start.6 = (pred[32]{0:T(512)(128)(4,1)S(1)}, pred[32]{0:T(512)(128)(4,1)}, u32[]{:S(2)}) copy-start(pred[32]{0:T(512)(128)(4,1)} %copy-done.4) | copy-start | bytes 100
  159.3 6.8 %copy-start.10 = (s32[32]{0:T(128)S(1)}, s32[32]{0:T(128)}, u32[]{:S(2)}) copy-start(s32[32]{0:T(128)} %copy-done.7) | copy-start | bytes 388
  159.3 6.8 %copy-start.15 = (pred[32]{0:T(512)(128)(4,1)S(1)}, pred[32]{0:T(512)(128)(4,1)}, u32[]{:S(2)}) copy-start(pred[32]{0:T(512)(128)(4,1)} %get-tuple-element.116) | copy-start | bytes 100
  169.7 2.7 %collective-permute-start.6 = (bf16[16,4,128]{2,0,1:T(8,128)(2,1)S(1)}, bf16[16,4,128]{2,0,1:T(8,128)(2,1)S(1)}, u32[]{:S(2)}, u32[]{:S(2)}) collective-permute-start(bf16[16,4,128]{2,0,1:T(8,128)(2,1)S(1)} %slice.221), channel_id=1, source_target_pairs={{0,4},{4,8},{8,12},{1,5},{5,9},{9,13},{2,6},{6,10},{10,14},{3,7},{... | collective-permute-start | bytes 49160 | tf_op jit(solution)/shard_map/ppermute | solution.py:14
  171.0 5.6 %collective-permute-start.7 = (bf16[16,4,128]{2,0,1:T(8,128)(2,1)S(1)}, bf16[16,4,128]{2,0,1:T(8,128)(2,1)S(1)}, u32[]{:S(2)}, u32[]{:S(2)}) collective-permute-start(bf16[16,4,128]{2,0,1:T(8,128)(2,1)S(1)} %slice.221), channel_id=1, source_target_pairs={{4,0},{8,4},{12,8},{5,1},{9,5},{13,9},{6,2},{10,6},{14,10},{7,3},{... | collective-permute-start | bytes 49160 | tf_op jit(solution)/shard_map/ppermute | solution.py:15
Sparse Core Ops, SparseCore 0:
  28.9 24.4 reduce-scatter.4
  77.5 21.7 reduce-scatter.6
  123.5 21.5 reduce-scatter.8
  168.5 21.5 reduce-scatter.10
where the time goes:
time: 216 us; the launch traced here: 214 us
  local copies, waits for them, and re-layouts  63.6 us (29%)
  waiting for transfers between devices  43.7 us (20%)
  matrix products  43.2 us (20%)
  blocking collectives  23.1 us (11%)
  starting transfers between devices  14.3 us (7%)
  between operations  14.1 us (7%)
  other arithmetic  12.2 us (6%)
    reduce_scatter x4, waiting for transfers between devices, body(): lax.psum_scatter(jnp.dot(match, slot_terms, precision=lax.Precision.HIGHE...  32.8 us
    psum x4, blocking collectives, body(): total_field = lax.psum(near_field + far_field, ('dir', 'sub'))  23.1 us
    dot_general x4, matrix products, body(): jnp.einsum('bnlst,bnlt->bs', near_blocks, partner_hist, preferred_element...  18.4 us
    scatter x4, local copies, waits for them, and re-layouts, body(): ray_buf = ray_buf.at[:, hist_len + moment].set(new_rays)  14.2 us
    reshape x4, local copies, waits for them, and re-layouts, body(): ray_table = ray_buf.reshape(box_count * buffer_len, ray_width)  14.1 us
    gather x4, local copies, waits for them, and re-layouts, body(): jnp.take(ray_table, row_ids, axis=0)  12.2 us
    ppermute x4, waiting for transfers between devices, padded(): after = lax.ppermute(leading, axis, down)  10.6 us
    ppermute x4, starting transfers between devices, padded(): before = lax.ppermute(last, axis, up)  8.76 us
  transfers between devices with their start and end apart: 12, of which 8 were waited for; matrix products, arithmetic and copies ran while one was open for 24% of the time, Pallas kernels for 0%

commit v1 on v0

v1 whole, which is shorter than its diff:
```python
import functools

import jax
import jax.numpy as jnp
from jax import lax
from jax.experimental import pallas as pl
from jax.experimental.pallas import tpu as pltpu
from jax.sharding import PartitionSpec as P

MESH = pl.DeviceIdType.MESH
NT_DIMS = (((1,), (1,)), ((), ()))
F32 = jnp.float32
BF16 = jnp.bfloat16


def march(
    peers,
    dirs,
    subs,
    hist_cur,
    hist_rays,
    incident,
    near_hbm,
    near_pick,
    inverse_hbm,
    projection,
    reception,
    translations,
    class_pick,
    hist_pick,
    new_pick,
    target_pick,
    out,
    near_v,
    inverse_v,
    inverse_cat,
    win,
    cur_all,
    factors,
    hist_terms,
    far_send,
    far_recv,
    part,
    near_sem,
    inverse_sem,
    win_send_sem,
    win_recv_sem,
    far_send_sem,
    far_recv_sem,
    part_send_sem,
    part_recv_sem,
):
    steps, boxes, width = incident.shape
    lag_span = hist_cur.shape[0]
    lags = near_v.shape[2]
    near = near_v.shape[1]
    rays = projection.shape[1]
    slots = class_pick.shape[0]
    spread = dirs * subs
    box = lax.axis_index("box")
    piece = lax.axis_index("dir") * subs + lax.axis_index("sub")
    chunk = 512 if rays % 512 == 0 else (256 if rays % 256 == 0 else 128)

    near_copy = pltpu.make_async_copy(near_hbm, near_v, near_sem)
    inverse_copy = pltpu.make_async_copy(inverse_hbm, inverse_v, inverse_sem)
    inverse_copy.start()
    near_copy.start()

    def peer_of(offset):
        return {"box": lax.rem(box + offset, peers)}

    def sibling_of(offset):
        other = lax.rem(piece + offset, spread)
        return {"dir": other // subs, "sub": lax.rem(other, subs)}

    win[1, pl.ds(0, lag_span)] = hist_cur[...]
    win[0] = jnp.zeros(win.shape[1:], F32)
    win[2] = jnp.zeros(win.shape[1:], F32)
    cur_all[...] = jnp.zeros(cur_all.shape, BF16)

    barrier = pltpu.get_barrier_semaphore()
    for offset in range(1, peers):
        pl.semaphore_signal(barrier, inc=1, device_id=peer_of(offset), device_id_type=MESH)
    for offset in range(1, spread):
        pl.semaphore_signal(barrier, inc=1, device_id=sibling_of(offset), device_id_type=MESH)

    pl.semaphore_wait(barrier, peers - 1 + spread - 1)

    def window_copy(order, side):
        span = pl.ds(0, lag_span) if order == 0 else pl.ds(lag_span + order - 1, 1)
        offset = 1 if side == 0 else peers - 1
        return pltpu.make_async_remote_copy(
            src_ref=win.at[1, span],
            dst_ref=win.at[0 if side == 0 else 2, span],
            send_sem=win_send_sem.at[order, side],
            recv_sem=win_recv_sem.at[order, side],
            device_id=peer_of(offset),
            device_id_type=MESH,
        )

    has_next = box < peers - 1
    has_prev = box > 0

    def start_window(order):
        @pl.when(has_next)
        def _():
            window_copy(order, 0).start()

        @pl.when(has_prev)
        def _():
            window_copy(order, 1).start()

    def wait_window(order):
        @pl.when(has_prev)
        def _():
            window_copy(order, 0).wait_recv()

        @pl.when(has_next)
        def _():
            window_copy(order, 1).wait_recv()

    def wait_window_sent(order):
        @pl.when(has_next)
        def _():
            window_copy(order, 0).wait_send()

        @pl.when(has_prev)
        def _():
            window_copy(order, 1).wait_send()

    start_window(0)

    def far_copy(step, offset):
        return pltpu.make_async_remote_copy(
            src_ref=far_send.at[step, lax.rem(box + offset, peers)],
            dst_ref=far_recv.at[step, offset],
            send_sem=far_send_sem.at[step, offset],
            recv_sem=far_recv_sem.at[step, offset],
            device_id=peer_of(offset),
            device_id_type=MESH,
        )

    def part_copy(step, offset):
        return pltpu.make_async_remote_copy(
            src_ref=part.at[step, piece],
            dst_ref=part.at[step, piece],
            send_sem=part_send_sem.at[step, offset],
            recv_sem=part_recv_sem.at[step, offset],
            device_id=sibling_of(offset),
            device_id_type=MESH,
        )

    def columns(index):
        return pl.ds(pl.multiple_of(index * chunk, chunk), chunk)

    def history_part(index, total):
        at = columns(index)
        factor = jnp.dot(class_pick[...], translations[:, at], preferred_element_type=F32).astype(BF16)
        factors[:, at] = factor
        picked = jnp.dot(hist_pick[...], hist_rays[:, at], preferred_element_type=F32).astype(BF16)
        terms = jnp.concatenate(
            [picked[t * slots : (t + 1) * slots] * factor for t in range(steps)], axis=0
        )
        return total + jnp.dot(terms, reception[at, :], preferred_element_type=F32)

    hist_terms[...] = lax.fori_loop(
        0, rays // chunk, history_part, jnp.zeros((steps * slots, width), F32)
    )

    def send_far(step):
        terms = hist_terms[pl.ds(step * slots, slots), :]
        if step > 0:
            picked = jnp.dot(
                new_pick[pl.ds(step * slots, slots), :], cur_all[...], preferred_element_type=F32
            ).astype(BF16)

            def new_part(index, total):
                at = columns(index)
                ray = jnp.dot(picked, projection[:, at], preferred_element_type=F32).astype(BF16)
                return total + jnp.dot(
                    ray * factors[:, at], reception[at, :], preferred_element_type=F32
                )

            terms = lax.fori_loop(0, rays // chunk, new_part, terms)
        far = jnp.dot(
            target_pick[...], terms, precision=lax.Precision.HIGHEST, preferred_element_type=F32
        )
        far_send[step] = far.reshape(peers, boxes, width)
        for offset in range(1, peers):
            far_copy(step, offset).start()

    row = lax.broadcasted_iota(jnp.int32, (boxes, width), 0)

    for step in range(steps):
        send_far(step)
        if step == 0:
            inverse_copy.wait()

            def split(index, carry):
                whole = inverse_v[index]
                high = whole.astype(BF16)
                low = (whole - high.astype(F32)).astype(BF16)
                inverse_cat[index] = jnp.concatenate([high, low], axis=1)
                return carry

            lax.fori_loop(0, boxes, split, 0)
            near_copy.wait()
        wait_window(step)

        pieces = []
        for lag in range(lags):
            at = lag_span + step - (piece * lags + lag + 1)
            table = jnp.concatenate([win[0, at], win[1, at], win[2, at]], axis=0).astype(BF16)
            gathered = jnp.dot(near_pick[...], table, preferred_element_type=F32).astype(BF16)
            for n in range(near):
                pieces.append(gathered[n * boxes : (n + 1) * boxes])
        sources = jnp.concatenate(pieces, axis=1)

        def near_part(index, total):
            blocks = jnp.concatenate(
                [near_v[index, n, lag] for lag in range(lags) for n in range(near)], axis=1
            )
            value = lax.dot_general(sources, blocks, NT_DIMS, preferred_element_type=F32)
            return total + jnp.where(row == index, value, 0.0)

        field = lax.fori_loop(0, boxes, near_part, jnp.zeros((boxes, width), F32))
        field = field + far_send[step, box]
        for offset in range(1, peers):
            far_copy(step, offset).wait_recv()
            field = field + far_recv[step, offset]
        part[step, piece] = field
        for offset in range(1, spread):
            part_copy(step, offset).start()
        for offset in range(1, spread):
            part_copy(step, offset).wait_recv()
        total = part[step, 0]
        for other in range(1, spread):
            total = total + part[step, other]

        drive = incident[step] - total
        high = drive.astype(BF16)
        low = (drive - high.astype(F32)).astype(BF16)
        left = jnp.concatenate(
            [
                jnp.concatenate([high, high], axis=1),
                jnp.concatenate([low, jnp.zeros_like(low)], axis=1),
            ],
            axis=0,
        )

        def solve_part(index, total):
            value = lax.dot_general(left, inverse_cat[index], NT_DIMS, preferred_element_type=F32)
            return total + jnp.where(row == index, value[:boxes] + value[boxes:], 0.0)

        current = lax.fori_loop(0, boxes, solve_part, jnp.zeros((boxes, width), F32)).astype(BF16)
        out[step] = current
        if step < steps - 1:
            cur_all[pl.ds(step * boxes, boxes), :] = current
            win[1, lag_span + step] = current.astype(F32)
            start_window(step + 1)

    for step in range(steps):
        wait_window_sent(step)
        for offset in range(1, peers):
            far_copy(step, offset).wait_send()
        for offset in range(1, spread):
            part_copy(step, offset).wait_send()


def body(
    history_currents,
    history_rays,
    incident,
    near_blocks,
    near_partners,
    self_inverse,
    projection,
    reception,
    translations,
    send_source,
    send_delay,
    send_target,
    send_class,
    slot_counts,
):
    boxes, hist_len, width = history_currents.shape
    rays = history_rays.shape[2]
    steps = incident.shape[1]
    near, lags = near_blocks.shape[1:3]
    peers, dirs, subs = (lax.axis_size(a) for a in ("box", "dir", "sub"))
    spread = dirs * subs
    lag_span = lags * spread
    box = lax.axis_index("box")
    capacity = send_source.shape[2]
    slots = peers * capacity
    classes = translations.shape[0]

    source = send_source.reshape(slots)
    delay = send_delay.reshape(slots)
    class_ids = send_class.reshape(slots)
    moment = jnp.arange(steps)[:, None]
    back = moment - delay[None, :]
    hist_row = jnp.where(back < 0, source * hist_len + hist_len + back, -1).reshape(-1, 1)
    new_row = jnp.where(back >= 0, back * boxes + source, -1).reshape(-1, 1)
    hist_pick = (hist_row == jnp.arange(boxes * hist_len)).astype(BF16)
    new_pick = (new_row == jnp.arange(steps * boxes)).astype(BF16)
    class_pick = (class_ids[:, None] == jnp.arange(classes)).astype(BF16)
    live = jnp.arange(capacity)[None, :] < slot_counts[0][:, None]
    dest = jnp.where(live, jnp.arange(peers)[:, None] * boxes + send_target[0], -1).reshape(1, slots)
    target_pick = (jnp.arange(peers * boxes)[:, None] == dest).astype(F32)
    local = (near_partners - (box - 1) * boxes).T.reshape(-1, 1)
    near_pick = (local == jnp.arange(3 * boxes)).astype(BF16)
    hist_cur = history_currents[:, hist_len - lag_span :].transpose(1, 0, 2).astype(F32)

    vmem = pl.BlockSpec(memory_space=pltpu.VMEM)
    hbm = pl.BlockSpec(memory_space=pl.ANY)
    dma = pltpu.SemaphoreType.DMA
    currents = pl.pallas_call(
        functools.partial(march, peers, dirs, subs),
        out_shape=jax.ShapeDtypeStruct((steps, boxes, width), BF16),
        in_specs=[vmem, vmem, vmem, hbm, vmem, hbm, vmem, vmem, vmem, vmem, vmem, vmem, vmem],
        out_specs=vmem,
        scratch_shapes=[
            pltpu.VMEM(near_blocks.shape, BF16),
            pltpu.VMEM(self_inverse.shape, F32),
            pltpu.VMEM((boxes, width, 2 * width), BF16),
            pltpu.VMEM((3, lag_span + steps, boxes, width), F32),
            pltpu.VMEM((steps * boxes, width), BF16),
            pltpu.VMEM((slots, rays), BF16),
            pltpu.VMEM((steps * slots, width), F32),
            pltpu.VMEM((steps, peers, boxes, width), F32),
            pltpu.VMEM((steps, peers, boxes, width), F32),
            pltpu.VMEM((steps, spread, boxes, width), F32),
            dma,
            dma,
            dma((steps, 2)),
            dma((steps, 2)),
            dma((steps, peers)),
            dma((steps, peers)),
            dma((steps, spread)),
            dma((steps, spread)),
        ],
        compiler_params=pltpu.CompilerParams(
            collective_id=0, has_side_effects=True, vmem_limit_bytes=48 * 1024 * 1024
        ),
    )(
        hist_cur,
        history_rays.reshape(boxes * hist_len, rays),
        incident.transpose(1, 0, 2),
        near_blocks,
        near_pick,
        self_inverse,
        projection,
        reception,
        translations,
        class_pick,
        hist_pick,
        new_pick,
        target_pick,
    )
    currents = currents.transpose(1, 0, 2)
    new_rays = jnp.einsum("bts,sk->btk", currents, projection, preferred_element_type=F32)
    return currents, new_rays.astype(BF16)


def solution(mesh):
    return jax.shard_map(
        body,
        mesh=mesh,
        in_specs=(
            P(("groups", "box"), None, None),
            P(("groups", "box"), None, ("dir", "sub")),
            P(("groups", "box"), None, None),
            P("box", None, ("dir", "sub"), None, None),
            P("box", None),
            P("box", None, None),
            P(None, ("dir", "sub")),
            P(("dir", "sub"), None),
            P(None, ("dir", "sub")),
            P("box", None, None),
            P("box", None, None),
            P("box", None, None),
            P("box", None, None),
            P("box", None),
        ),
        out_specs=(P(("groups", "box"), None, None), P(("groups", "box"), None, ("dir", "sub"))),
        check_vma=False,
    )
```

time: 216 us -> 68.1 us (0.32)
  Pallas kernels: 0 us -> 51.8 us
  local copies, waits for them, and re-layouts: 63.6 us -> 12.9 us
  waiting for transfers between devices: 43.7 us -> 0 us
  matrix products: 43.2 us -> 0.23 us
  blocking collectives: 23.1 us -> 0 us
  starting transfers between devices: 14.3 us -> 0 us
  between operations: 14.1 us -> 0.72 us
  other arithmetic: 12.2 us -> 1.8 us
    pallas_call x0 -> x1, Pallas kernels: none -> 51.8 us  [body(): pl.pallas_call(functools.partial(march, peers, dirs, subs), out_shape=jax...]
    dot_general x20 -> x1, matrix products: 43.2 us -> 0.23 us  [body(): jnp.einsum('bts,sk->btk', currents, projection, preferred_element_type=F32)]
    reduce_scatter x4 -> x0, waiting for transfers between devices: 32.8 us -> none  [body(): lax.psum_scatter(jnp.dot(match, slot_terms, precision=lax.Precision.HIGHE...]
    psum x4 -> x0, blocking collectives: 23.1 us -> none  [body(): total_field = lax.psum(near_field + far_field, ('dir', 'sub'))]
    gather x13 -> x0, local copies, waits for them, and re-layouts: 20.1 us -> none  [the longest x4 12.2 us: body(): jnp.take(ray_table, row_ids, axis=0)]
    scatter x4 -> x0, local copies, waits for them, and re-layouts: 14.2 us -> none  [body(): ray_buf = ray_buf.at[:, hist_len + moment].set(new_rays)]
    ppermute x8 -> x0, starting transfers between devices: 14.1 us -> none  [the longest x4 8.76 us: padded(): before = lax.ppermute(last, axis, up)]
    reshape x4 -> x1, local copies, waits for them, and re-layouts: 14.1 us -> 0.76 us  [body(): source = send_source.reshape(slots)]
  transfers between devices with their start and end apart: 12 -> 0, of which waited for: 8 -> 0; matrix products, arithmetic and copies ran while one was open for 24% -> 0% of each run, Pallas kernels for 0% -> 0%
where the time goes in v1:
time: 68.1 us; the launch traced here: 67.5 us
  Pallas kernels  51.8 us (76%)
  local copies, waits for them, and re-layouts  12.9 us (19%)
  other arithmetic  1.8 us (3%)
  between operations  0.72 us (1%)
    pallas_call x1, Pallas kernels, body(): pl.pallas_call(functools.partial(march, peers, dirs, subs), out_shape=jax...  51.8 us
    unnamed x13, local copies, waits for them, and re-layouts  8.49 us

profile of v1, /device:TPU:0, one launch (start us, length us, event | category | flops | bytes accessed | tf_op | source)
XLA Modules:
  0.0 67.5 jit_solution(5191909103458797450)
XLA Ops:
  0.6 0.8 %reshape.112 = s32[32]{0:T(128)S(1)} reshape(s32[1,4,8]{2,1,0:T(4,128)} %param.23) | data formatting | bytes 256 | tf_op jit(solution)/shard_map/reshape | solution.py:298
  1.4 0.8 %sub.36 = s32[32]{0:T(128)S(1)} reshape(s32[1,4,8]{2,1,0:T(4,128)} %param.24) | data formatting | bytes 256 | tf_op jit(solution)/shard_map/sub | solution.py:302
  2.2 0.8 %squeeze.3 = s32[32]{0:T(128)S(1)} reshape(s32[1,4,8]{2,1,0:T(4,128)} %param.25) | data formatting | bytes 256 | tf_op jit(solution)/shard_map/squeeze | solution.py:309
  2.9 0.8 %eq.73 = s32[32]{0:T(128)S(1)} reshape(s32[1,4,8]{2,1,0:T(4,128)} %param.26) | data formatting | bytes 256 | tf_op jit(solution)/shard_map/eq | solution.py:307
  3.7 0.7 %iota_compare_fusion.5 = pred[4,8]{1,0:T(4,128)(4,1)S(1)} fusion(s32[4]{0:T(128)} %bitcast.18), kind=kLoop, calls=%fused_computation.15 | loop fusion | flops 32 | bytes 48 | tf_op jit(solution)/shard_map/lt | solution.py:308
  4.4 0.1 lt.35
  4.5 0.1 add.53
  4.6 0.1 add.54
  4.7 0.1 select_n.32
  4.8 0.1 select_n.30
  4.9 0.7 %subtract_bitcast_fusion = s32[12,16]{0,1:T(8,128)S(1)} fusion(s32[16,12]{1,0:T(8,128)} %param.18, s32[]{:T(128)S(6)} %mul.29), kind=kLoop, calls=%fused_computation.14 | loop fusion | flops 192 | bytes 1540 | tf_op jit(solution)/shard_map/transpose | solution.py:311
  5.6 0.1 copy.22
  5.7 0.1 eq.34
  5.7 0.8 %slice.3 = bf16[16,4,128]{2,1,0:T(4,128)(2,1)S(1)} slice(bf16[16,16,128]{2,1,0:T(8,128)(2,1)} %param.14), slice={[0:16], [12:16], [0:128]} | slice | bytes 32768 | tf_op jit(solution)/shard_map/slice | solution.py:313
  6.5 0.1 fusion.4.class_pick
  6.6 0.1 fusion.3.new_pick
  6.7 0.8 %copy.28 = f32[16,4,128]{2,0,1:T(8,128)S(1)} copy(f32[16,4,128]{2,1,0:T(4,128)} %param.16) | data formatting | bytes 65536 | tf_op args[2]
  7.5 0.1 fusion.2.near_pick
  7.6 0.1 fusion.1.hist_pick
  7.7 0.0 copy-start
  7.7 1.1 %copy-done = bf16[128,2560]{1,0:T(8,128)(2,1)S(1)} copy-done((bf16[128,2560]{1,0:T(8,128)(2,1)S(1)}, bf16[128,2560]{1,0:T(8,128)(2,1)}, u32[]{:S(2)}) %copy-start) | copy-done | bytes 655384
  8.7 0.0 copy-start.1
  8.7 1.4 %copy-done.1 = bf16[316,2560]{1,0:T(8,128)(2,1)S(1)} copy-done((bf16[316,2560]{1,0:T(8,128)(2,1)S(1)}, bf16[316,2560]{1,0:T(8,128)(2,1)}, u32[]{:S(2)}) %copy-start.1) | copy-done | bytes 1617944
  10.2 0.0 copy-start.2
  10.2 1.3 %copy-done.2 = bf16[16,16,2560]{2,1,0:T(8,128)(2,1)S(1)} copy-done((bf16[16,16,2560]{2,1,0:T(8,128)(2,1)S(1)}, bf16[16,16,2560]{2,1,0:T(8,128)(2,1)}, u32[]{:S(2)}) %copy-start.2) | copy-done | bytes 1310744
  11.5 0.0 copy-start.3
  11.5 1.2 %copy-done.3 = f32[16,128,128]{2,1,0:T(8,128)S(1)} copy-done((f32[16,128,128]{2,1,0:T(8,128)S(1)}, f32[16,128,128]{2,1,0:T(8,128)}, u32[]{:S(2)}) %copy-start.3) | copy-done | bytes 1048600
  12.7 0.0 copy-start.4
  12.7 1.1 %copy-done.4 = bf16[2560,128]{1,0:T(8,128)(2,1)S(1)} copy-done((bf16[2560,128]{1,0:T(8,128)(2,1)S(1)}, bf16[2560,128]{1,0:T(8,128)(2,1)}, u32[]{:S(2)}) %copy-start.4) | copy-done | bytes 655384
  13.8 51.8 %shard_map.149 = bf16[4,16,128]{2,1,0:T(8,128)(2,1)S(1)} custom-call(f32[4,16,128]{2,1,0:T(8,128)S(1)} %convert_bitcast_fusion.hist_cur, bf16[256,2560]{1,0:T(8,128)(2,1)S(1)} %bitcast.15, f32[4,16,128]{2,1,0:T(8,128)S(1)} %bitcast.17, bf16[16,12,1,128,128]{4,3,2,1,0:T(8,128)(2,1)} %near_hbm.1, bf16[192,48]{1,0:T(8,128)(2,1)S(1)} %fusion.2.near_pick, ...), custom_call_target="tpu_custom_call" | custom-call | tf_op jit(solution)/shard_map/pallas_call | solution.py:318
  65.7 0.6 copy.23
  66.3 0.2 convolution_convert_fusion
  66.5 1.0 %copy.24 = bf16[16,4,2560]{2,1,0:T(4,128)(2,1)} copy(bf16[16,4,2560]{2,0,1:T(8,128)(2,1)S(1)} %convolution_convert_fusion) | data formatting | bytes 655360
  (6 shorter events, 0.0 us)
Async XLA Ops:
  7.7 1.1 %copy-start = (bf16[128,2560]{1,0:T(8,128)(2,1)S(1)}, bf16[128,2560]{1,0:T(8,128)(2,1)}, u32[]{:S(2)}) copy-start(bf16[128,2560]{1,0:T(8,128)(2,1)} %projection.1) | copy-start | bytes 1966084
  8.7 1.4 %copy-start.1 = (bf16[316,2560]{1,0:T(8,128)(2,1)S(1)}, bf16[316,2560]{1,0:T(8,128)(2,1)}, u32[]{:S(2)}) copy-start(bf16[316,2560]{1,0:T(8,128)(2,1)} %translations.1) | copy-start | bytes 4853764
  10.2 1.3 %copy-start.2 = (bf16[16,16,2560]{2,1,0:T(8,128)(2,1)S(1)}, bf16[16,16,2560]{2,1,0:T(8,128)(2,1)}, u32[]{:S(2)}) copy-start(bf16[16,16,2560]{2,1,0:T(8,128)(2,1)} %param.15) | copy-start | bytes 3932164
  11.5 1.2 %copy-start.3 = (f32[16,128,128]{2,1,0:T(8,128)S(1)}, f32[16,128,128]{2,1,0:T(8,128)}, u32[]{:S(2)}) copy-start(f32[16,128,128]{2,1,0:T(8,128)} %inverse_hbm.1) | copy-start | bytes 3145732
  12.7 1.1 %copy-start.4 = (bf16[2560,128]{1,0:T(8,128)(2,1)S(1)}, bf16[2560,128]{1,0:T(8,128)(2,1)}, u32[]{:S(2)}) copy-start(bf16[2560,128]{1,0:T(8,128)(2,1)} %reception.1) | copy-start | bytes 1966084

commit v2 on v1

--- a/solution.py
+++ b/solution.py
@@ -17,32 +17,40 @@
     peers,
     dirs,
     subs,
+    source_ids,
+    delay_ids,
+    target_ids,
+    class_ids,
+    live_counts,
+    partner_ids,
     hist_cur,
+    incident,
+    rays_hbm,
+    near_hbm,
+    inverse_hbm,
+    projection_hbm,
+    reception_hbm,
+    translations_hbm,
+    out,
     hist_rays,
-    incident,
-    near_hbm,
-    near_pick,
-    inverse_hbm,
+    near_v,
+    inverse_v,
     projection,
     reception,
     translations,
-    class_pick,
-    hist_pick,
+    inverse_cat,
+    hist_f32,
+    win,
+    cur_all,
+    near_pick,
     new_pick,
     target_pick,
-    out,
-    near_v,
-    inverse_v,
-    inverse_cat,
-    win,
-    cur_all,
     factors,
     hist_terms,
     far_send,
     far_recv,
     part,
-    near_sem,
-    inverse_sem,
+    copy_sems,
     win_send_sem,
     win_recv_sem,
     far_send_sem,
@@ -50,21 +58,34 @@
     part_send_sem,
     part_recv_sem,
 ):
-    steps, boxes, width = incident.shape
-    lag_span = hist_cur.shape[0]
+    boxes, steps, width = incident.shape
+    hist_len = hist_cur.shape[1]
     lags = near_v.shape[2]
     near = near_v.shape[1]
     rays = projection.shape[1]
-    slots = class_pick.shape[0]
+    capacity = source_ids.shape[2]
+    slots = peers * capacity
     spread = dirs * subs
+    lag_span = lags * spread
     box = lax.axis_index("box")
     piece = lax.axis_index("dir") * subs + lax.axis_index("sub")
     chunk = 512 if rays % 512 == 0 else (256 if rays % 256 == 0 else 128)
 
-    near_copy = pltpu.make_async_copy(near_hbm, near_v, near_sem)
-    inverse_copy = pltpu.make_async_copy(inverse_hbm, inverse_v, inverse_sem)
-    inverse_copy.start()
-    near_copy.start()
+    copies = [
+        pltpu.make_async_copy(src, dst, copy_sems.at[i])
+        for i, (src, dst) in enumerate(
+            (
+                (translations_hbm, translations),
+                (rays_hbm, hist_rays),
+                (reception_hbm, reception),
+                (inverse_hbm, inverse_v),
+                (near_hbm, near_v),
+                (projection_hbm, projection),
+            )
+        )
+    ]
+    for copy in copies:
+        copy.start()
 
     def peer_of(offset):
         return {"box": lax.rem(box + offset, peers)}
@@ -73,7 +94,9 @@
         other = lax.rem(piece + offset, spread)
         return {"dir": other // subs, "sub": lax.rem(other, subs)}
 
-    win[1, pl.ds(0, lag_span)] = hist_cur[...]
+    hist_f32[...] = hist_cur[...].astype(F32)
+    for back in range(lag_span):
+        win[1, back] = hist_f32[:, hist_len - lag_span + back, :]
     win[0] = jnp.zeros(win.shape[1:], F32)
     win[2] = jnp.zeros(win.shape[1:], F32)
     cur_all[...] = jnp.zeros(cur_all.shape, BF16)
@@ -84,6 +107,40 @@
     for offset in range(1, spread):
         pl.semaphore_signal(barrier, inc=1, device_id=sibling_of(offset), device_id_type=MESH)
 
+
+    def column_of(count, value):
+        tiles = []
+        rows = lax.broadcasted_iota(jnp.int32, (8, 1), 0)
+        for start in range(0, count, 8):
+            tile = jnp.full((8, 1), -1, jnp.int32)
+            for i in range(min(8, count - start)):
+                tile = jnp.where(rows == i, value(start + i), tile)
+            tiles.append(tile)
+        return jnp.concatenate(tiles, axis=0)[:count]
+
+    def pick(ids, size):
+        lanes = lax.broadcasted_iota(jnp.int32, (ids.shape[0], size), 1)
+        return jnp.where(lanes == ids, 1.0, 0.0)
+
+    def slot_of(ref):
+        return column_of(slots, lambda j: ref[0, j // capacity, j % capacity])
+
+    source, delay = slot_of(source_ids), slot_of(delay_ids)
+    hist_rows = []
+    new_rows = []
+    for step in range(steps):
+        back = step - delay
+        hist_rows.append(jnp.where(back < 0, source * hist_len + hist_len + back, -1))
+        new_rows.append(jnp.where(back >= 0, back * boxes + source, -1))
+    hist_pick = pick(jnp.concatenate(hist_rows, axis=0), boxes * hist_len).astype(BF16)
+    new_pick[...] = pick(jnp.concatenate(new_rows, axis=0), steps * boxes).astype(BF16)
+    class_pick = pick(slot_of(class_ids), translations.shape[0]).astype(BF16)
+    live = column_of(slots, lambda j: live_counts[0, j // capacity])
+    place = lax.broadcasted_iota(jnp.int32, (slots, 1), 0)
+    dest = jnp.where(place % capacity < live, place // capacity * boxes + slot_of(target_ids), -1)
+    target_pick[...] = pick(dest, peers * boxes)
+    partner = column_of(near * boxes, lambda j: partner_ids[j % boxes, j // boxes])
+    near_pick[...] = pick(partner - (box - 1) * boxes, 3 * boxes).astype(BF16)
     pl.semaphore_wait(barrier, peers - 1 + spread - 1)
 
     def window_copy(order, side):
@@ -151,21 +208,24 @@
         )
 
     def columns(index):
-        return pl.ds(pl.multiple_of(index * chunk, chunk), chunk)
+        return pl.ds(index * chunk, chunk)
 
     def history_part(index, total):
         at = columns(index)
-        factor = jnp.dot(class_pick[...], translations[:, at], preferred_element_type=F32).astype(BF16)
+        factor = jnp.dot(class_pick, translations[:, at], preferred_element_type=F32).astype(BF16)
         factors[:, at] = factor
-        picked = jnp.dot(hist_pick[...], hist_rays[:, at], preferred_element_type=F32).astype(BF16)
+        picked = jnp.dot(hist_pick, hist_rays[:, at], preferred_element_type=F32).astype(BF16)
         terms = jnp.concatenate(
             [picked[t * slots : (t + 1) * slots] * factor for t in range(steps)], axis=0
         )
         return total + jnp.dot(terms, reception[at, :], preferred_element_type=F32)
 
-    hist_terms[...] = lax.fori_loop(
-        0, rays // chunk, history_part, jnp.zeros((steps * slots, width), F32)
-    )
+    for copy in copies[:3]:
+        copy.wait()
+    total = jnp.zeros((steps * slots, width), F32)
+    for index in range(rays // chunk):
+        total = history_part(index, total)
+    hist_terms[...] = total
 
     def send_far(step):
         terms = hist_terms[pl.ds(step * slots, slots), :]
@@ -181,9 +241,14 @@
                     ray * factors[:, at], reception[at, :], preferred_element_type=F32
                 )
 
-            terms = lax.fori_loop(0, rays // chunk, new_part, terms)
-        far = jnp.dot(
-            target_pick[...], terms, precision=lax.Precision.HIGHEST, preferred_element_type=F32
+            for index in range(rays // chunk):
+                terms = new_part(index, terms)
+        far = lax.dot_general(
+            target_pick[...],
+            terms,
+            (((0,), (0,)), ((), ())),
+            precision=lax.Precision.HIGHEST,
+            preferred_element_type=F32,
         )
         far_send[step] = far.reshape(peers, boxes, width)
         for offset in range(1, peers):
@@ -194,7 +259,7 @@
     for step in range(steps):
         send_far(step)
         if step == 0:
-            inverse_copy.wait()
+            copies[3].wait()
 
             def split(index, carry):
                 whole = inverse_v[index]
@@ -204,7 +269,8 @@
                 return carry
 
             lax.fori_loop(0, boxes, split, 0)
-            near_copy.wait()
+            copies[4].wait()
+            copies[5].wait()
         wait_window(step)
 
         pieces = []
@@ -223,7 +289,9 @@
             value = lax.dot_general(sources, blocks, NT_DIMS, preferred_element_type=F32)
             return total + jnp.where(row == index, value, 0.0)
 
-        field = lax.fori_loop(0, boxes, near_part, jnp.zeros((boxes, width), F32))
+        field = jnp.zeros((boxes, width), F32)
+        for index in range(boxes):
+            field = near_part(index, field)
         field = field + far_send[step, box]
         for offset in range(1, peers):
             far_copy(step, offset).wait_recv()
@@ -237,7 +305,7 @@
         for other in range(1, spread):
             total = total + part[step, other]
 
-        drive = incident[step] - total
+        drive = incident[:, step, :] - total
         high = drive.astype(BF16)
         low = (drive - high.astype(F32)).astype(BF16)
         left = jnp.concatenate(
@@ -252,7 +320,10 @@
             value = lax.dot_general(left, inverse_cat[index], NT_DIMS, preferred_element_type=F32)
             return total + jnp.where(row == index, value[:boxes] + value[boxes:], 0.0)
 
-        current = lax.fori_loop(0, boxes, solve_part, jnp.zeros((boxes, width), F32)).astype(BF16)
+        current = jnp.zeros((boxes, width), F32)
+        for index in range(boxes):
+            current = solve_part(index, current)
+        current = current.astype(BF16)
         out[step] = current
         if step < steps - 1:
             cur_all[pl.ds(step * boxes, boxes), :] = current
@@ -290,49 +361,36 @@
     peers, dirs, subs = (lax.axis_size(a) for a in ("box", "dir", "sub"))
     spread = dirs * subs
     lag_span = lags * spread
-    box = lax.axis_index("box")
-    capacity = send_source.shape[2]
-    slots = peers * capacity
-    classes = translations.shape[0]
-
-    source = send_source.reshape(slots)
-    delay = send_delay.reshape(slots)
-    class_ids = send_class.reshape(slots)
-    moment = jnp.arange(steps)[:, None]
-    back = moment - delay[None, :]
-    hist_row = jnp.where(back < 0, source * hist_len + hist_len + back, -1).reshape(-1, 1)
-    new_row = jnp.where(back >= 0, back * boxes + source, -1).reshape(-1, 1)
-    hist_pick = (hist_row == jnp.arange(boxes * hist_len)).astype(BF16)
-    new_pick = (new_row == jnp.arange(steps * boxes)).astype(BF16)
-    class_pick = (class_ids[:, None] == jnp.arange(classes)).astype(BF16)
-    live = jnp.arange(capacity)[None, :] < slot_counts[0][:, None]
-    dest = jnp.where(live, jnp.arange(peers)[:, None] * boxes + send_target[0], -1).reshape(1, slots)
-    target_pick = (jnp.arange(peers * boxes)[:, None] == dest).astype(F32)
-    local = (near_partners - (box - 1) * boxes).T.reshape(-1, 1)
-    near_pick = (local == jnp.arange(3 * boxes)).astype(BF16)
-    hist_cur = history_currents[:, hist_len - lag_span :].transpose(1, 0, 2).astype(F32)
-
+    slots = peers * send_source.shape[2]
+    smem = pl.BlockSpec(memory_space=pltpu.SMEM)
     vmem = pl.BlockSpec(memory_space=pltpu.VMEM)
     hbm = pl.BlockSpec(memory_space=pl.ANY)
     dma = pltpu.SemaphoreType.DMA
     currents = pl.pallas_call(
         functools.partial(march, peers, dirs, subs),
         out_shape=jax.ShapeDtypeStruct((steps, boxes, width), BF16),
-        in_specs=[vmem, vmem, vmem, hbm, vmem, hbm, vmem, vmem, vmem, vmem, vmem, vmem, vmem],
+        in_specs=[smem] * 6 + [vmem] * 2 + [hbm] * 6,
         out_specs=vmem,
         scratch_shapes=[
+            pltpu.VMEM((boxes * hist_len, rays), BF16),
             pltpu.VMEM(near_blocks.shape, BF16),
             pltpu.VMEM(self_inverse.shape, F32),
+            pltpu.VMEM(projection.shape, BF16),
+            pltpu.VMEM(reception.shape, BF16),
+            pltpu.VMEM(translations.shape, BF16),
             pltpu.VMEM((boxes, width, 2 * width), BF16),
+            pltpu.VMEM((boxes, hist_len, width), F32),
             pltpu.VMEM((3, lag_span + steps, boxes, width), F32),
             pltpu.VMEM((steps * boxes, width), BF16),
+            pltpu.VMEM((near * boxes, 3 * boxes), BF16),
+            pltpu.VMEM((steps * slots, steps * boxes), BF16),
+            pltpu.VMEM((slots, peers * boxes), F32),
             pltpu.VMEM((slots, rays), BF16),
             pltpu.VMEM((steps * slots, width), F32),
             pltpu.VMEM((steps, peers, boxes, width), F32),
             pltpu.VMEM((steps, peers, boxes, width), F32),
             pltpu.VMEM((steps, spread, boxes, width), F32),
-            dma,
-            dma,
+            dma((6,)),
             dma((steps, 2)),
             dma((steps, 2)),
             dma((steps, peers)),
@@ -341,22 +399,23 @@
             dma((steps, spread)),
         ],
         compiler_params=pltpu.CompilerParams(
-            collective_id=0, has_side_effects=True, vmem_limit_bytes=48 * 1024 * 1024
+            collective_id=0, has_side_effects=True, vmem_limit_bytes=60 * 1024 * 1024
         ),
     )(
-        hist_cur,
+        send_source,
+        send_delay,
+        send_target,
+        send_class,
+        slot_counts,
+        near_partners,
+        history_currents,
+        incident,
         history_rays.reshape(boxes * hist_len, rays),
-        incident.transpose(1, 0, 2),
         near_blocks,
-        near_pick,
         self_inverse,
         projection,
         reception,
         translations,
-        class_pick,
-        hist_pick,
-        new_pick,
-        target_pick,
     )
     currents = currents.transpose(1, 0, 2)
     new_rays = jnp.einsum("bts,sk->btk", currents, projection, preferred_element_type=F32)

time: 68.1 us -> 43.2 us (0.63)
  Pallas kernels: 51.8 us -> 39 us
  local copies, waits for them, and re-layouts: 12.9 us -> 2.31 us
  other arithmetic: 1.8 us -> 0 us
  matrix products: 0.23 us -> 0.95 us
    pallas_call x1, Pallas kernels: 51.8 us -> 39 us  [body(): pl.pallas_call(functools.partial(march, peers, dirs, subs), out_shape=jax...]
    unnamed x13 -> x4, local copies, waits for them, and re-layouts: 8.49 us -> 2.31 us
    eq x2 -> x0, local copies, waits for them, and re-layouts: 0.84 us -> none  [the longest x1 0.76 us: body(): class_pick = (class_ids[:, None] == jnp.arange(classes)).astype(BF16)]
    slice x1 -> x0, local copies, waits for them, and re-layouts: 0.77 us -> none  [body(): history_currents[:, hist_len - lag_span:].transpose(1, 0, 2).astype(F32)]
    reshape x1 -> x0, local copies, waits for them, and re-layouts: 0.76 us -> none  [body(): source = send_source.reshape(slots)]
    squeeze x1 -> x0, local copies, waits for them, and re-layouts: 0.76 us -> none  [body(): send_target[0]]
    sub x1 -> x0, local copies, waits for them, and re-layouts: 0.76 us -> none  [body(): back = moment - delay[None, :]]
    lt x1 -> x0, other arithmetic: 0.73 us -> none  [body(): live = jnp.arange(capacity)[None, :] < slot_counts[0][:, None]]
where the time goes in v2:
time: 43.2 us; the launch traced here: 42.9 us
  Pallas kernels  39 us (90%)
  local copies, waits for them, and re-layouts  2.31 us (5%)
  matrix products  0.95 us (2%)
  between operations  0.66 us (2%)
    pallas_call x1, Pallas kernels, body(): pl.pallas_call(functools.partial(march, peers, dirs, subs), out_shape=jax...  39 us
    unnamed x4, local copies, waits for them, and re-layouts  2.31 us
    dot_general x1, matrix products, body(): jnp.einsum('bts,sk->btk', currents, projection, preferred_element_type=F32)  0.95 us

profile of v2, /device:TPU:0, one launch (start us, length us, event | category | flops | bytes accessed | tf_op | source)
XLA Modules:
  0.0 42.9 jit_solution(14004851271156941587)
XLA Ops:
  0.6 0.0 copy-start
  0.6 39.0 %shard_map.149 = bf16[4,16,128]{2,1,0:T(8,128)(2,1)} custom-call(s32[1,4,8]{2,1,0:T(4,128)} %source_ids.1, s32[1,4,8]{2,1,0:T(4,128)} %delay_ids.1, s32[1,4,8]{2,1,0:T(4,128)} %target_ids.1, s32[1,4,8]{2,1,0:T(4,128)} %class_ids.1, s32[1,4]{1,0:T(1,128)} %live_counts.1, s32[16,12]{1,0:T(8,128)} %partner_ids.1, bf16[16,16,128]{2,1,0:T(8,128)(2,1)} %hist_cur.1, ...), custom_call_target="tpu_custom_call" | custom-call | tf_op jit(solution)/shard_map/pallas_call | solution.py:369
  39.6 1.3 %copy.16 = bf16[16,4,128]{2,1,0:T(4,128)(2,1)} copy(bf16[16,4,128]{2,0,1:T(8,128)(2,1)} %bitcast.8) | data formatting | bytes 32768
  41.0 0.0 copy-done
  41.0 0.9 %convolution_convert_fusion = bf16[16,4,2560]{2,0,1:T(8,128)(2,1)S(1)} fusion(bf16[128,2560]{1,0:T(8,128)(2,1)S(1)} %copy-done, bf16[4,16,128]{2,1,0:T(8,128)(2,1)} %shard_map.149), kind=kOutput, calls=%fused_computation | convolution fusion | flops 42106880 | bytes 999424 | tf_op jit(solution)/shard_map/bts,sk->btk/dot_general | solution.py:421
  41.9 1.0 %copy.17 = bf16[16,4,2560]{2,1,0:T(4,128)(2,1)} copy(bf16[16,4,2560]{2,0,1:T(8,128)(2,1)S(1)} %convolution_convert_fusion) | data formatting | bytes 655360
Async XLA Ops:
  0.6 40.3 %copy-start = (bf16[128,2560]{1,0:T(8,128)(2,1)S(1)}, bf16[128,2560]{1,0:T(8,128)(2,1)}, u32[]{:S(2)}) copy-start(bf16[128,2560]{1,0:T(8,128)(2,1)} %projection_hbm.1) | copy-start | bytes 1966084

commit v3 on v2

--- a/solution.py
+++ b/solution.py
@@ -34,6 +34,7 @@
     out,
     hist_rays,
     near_v,
+    near_t,
     inverse_v,
     projection,
     reception,
@@ -84,7 +85,7 @@
             )
         )
     ]
-    for copy in copies:
+    for copy in copies[:3]:
         copy.start()
 
     def peer_of(offset):
@@ -138,9 +139,12 @@
     live = column_of(slots, lambda j: live_counts[0, j // capacity])
     place = lax.broadcasted_iota(jnp.int32, (slots, 1), 0)
     dest = jnp.where(place % capacity < live, place // capacity * boxes + slot_of(target_ids), -1)
-    target_pick[...] = pick(dest, peers * boxes)
+    chosen = pick(dest, peers * boxes)
+    target_pick[...] = jnp.concatenate([chosen, chosen], axis=0).T.astype(BF16)
     partner = column_of(near * boxes, lambda j: partner_ids[j % boxes, j // boxes])
     near_pick[...] = pick(partner - (box - 1) * boxes, 3 * boxes).astype(BF16)
+    for copy in copies[3:]:
+        copy.start()
     pl.semaphore_wait(barrier, peers - 1 + spread - 1)
 
     def window_copy(order, side):
@@ -243,12 +247,10 @@
 
             for index in range(rays // chunk):
                 terms = new_part(index, terms)
-        far = lax.dot_general(
-            target_pick[...],
-            terms,
-            (((0,), (0,)), ((), ())),
-            precision=lax.Precision.HIGHEST,
-            preferred_element_type=F32,
+        high = terms.astype(BF16)
+        low = (terms - high.astype(F32)).astype(BF16)
+        far = jnp.dot(
+            target_pick[...], jnp.concatenate([high, low], axis=0), preferred_element_type=F32
         )
         far_send[step] = far.reshape(peers, boxes, width)
         for offset in range(1, peers):
@@ -262,10 +264,10 @@
             copies[3].wait()
 
             def split(index, carry):
-                whole = inverse_v[index]
+                whole = inverse_v[index].T
                 high = whole.astype(BF16)
                 low = (whole - high.astype(F32)).astype(BF16)
-                inverse_cat[index] = jnp.concatenate([high, low], axis=1)
+                inverse_cat[index] = jnp.concatenate([high, low], axis=0)
                 return carry
 
             lax.fori_loop(0, boxes, split, 0)
@@ -283,6 +285,9 @@
         sources = jnp.concatenate(pieces, axis=1)
 
         def near_part(index, total):
+            if step > 0:
+                value = jnp.dot(sources, near_t[index], preferred_element_type=F32)
+                return total + jnp.where(row == index, value, 0.0)
             blocks = jnp.concatenate(
                 [near_v[index, n, lag] for lag in range(lags) for n in range(near)], axis=1
             )
@@ -299,6 +304,16 @@
         part[step, piece] = field
         for offset in range(1, spread):
             part_copy(step, offset).start()
+        if step == 0:
+
+            def turn(index, carry):
+                for lag in range(lags):
+                    for n in range(near):
+                        start = (lag * near + n) * width
+                        near_t[index, pl.ds(start, width), :] = near_v[index, n, lag].T
+                return carry
+
+            lax.fori_loop(0, boxes, turn, 0)
         for offset in range(1, spread):
             part_copy(step, offset).wait_recv()
         total = part[step, 0]
@@ -317,7 +332,7 @@
         )
 
         def solve_part(index, total):
-            value = lax.dot_general(left, inverse_cat[index], NT_DIMS, preferred_element_type=F32)
+            value = jnp.dot(left, inverse_cat[index], preferred_element_type=F32)
             return total + jnp.where(row == index, value[:boxes] + value[boxes:], 0.0)
 
         current = jnp.zeros((boxes, width), F32)
@@ -374,17 +389,18 @@
         scratch_shapes=[
             pltpu.VMEM((boxes * hist_len, rays), BF16),
             pltpu.VMEM(near_blocks.shape, BF16),
+            pltpu.VMEM((boxes, lags * near * width, width), BF16),
             pltpu.VMEM(self_inverse.shape, F32),
             pltpu.VMEM(projection.shape, BF16),
             pltpu.VMEM(reception.shape, BF16),
             pltpu.VMEM(translations.shape, BF16),
-            pltpu.VMEM((boxes, width, 2 * width), BF16),
+            pltpu.VMEM((boxes, 2 * width, width), BF16),
             pltpu.VMEM((boxes, hist_len, width), F32),
             pltpu.VMEM((3, lag_span + steps, boxes, width), F32),
             pltpu.VMEM((steps * boxes, width), BF16),
             pltpu.VMEM((near * boxes, 3 * boxes), BF16),
             pltpu.VMEM((steps * slots, steps * boxes), BF16),
-            pltpu.VMEM((slots, peers * boxes), F32),
+            pltpu.VMEM((peers * boxes, 2 * slots), BF16),
             pltpu.VMEM((slots, rays), BF16),
             pltpu.VMEM((steps * slots, width), F32),
             pltpu.VMEM((steps, peers, boxes, width), F32),

time: 43.2 us -> 42.8 us (level)
  no operation moved by 1% of the time
where the time goes in v3:
time: 42.8 us; the launch traced here: 42.5 us
  Pallas kernels  38.6 us (90%)
  local copies, waits for them, and re-layouts  2.31 us (5%)
  matrix products  0.95 us (2%)
  between operations  0.66 us (2%)
    pallas_call x1, Pallas kernels, body(): pl.pallas_call(functools.partial(march, peers, dirs, subs), out_shape=jax...  38.6 us
    unnamed x4, local copies, waits for them, and re-layouts  2.31 us
    dot_general x1, matrix products, body(): jnp.einsum('bts,sk->btk', currents, projection, preferred_element_type=F32)  0.95 us

profile of v3, /device:TPU:0, one launch (start us, length us, event | category | flops | bytes accessed | tf_op | source)
XLA Modules:
  0.0 42.5 jit_solution(2163273133495271250)
XLA Ops:
  0.6 0.0 copy-start
  0.6 38.6 %shard_map.149 = bf16[4,16,128]{2,1,0:T(8,128)(2,1)} custom-call(s32[1,4,8]{2,1,0:T(4,128)} %source_ids.1, s32[1,4,8]{2,1,0:T(4,128)} %delay_ids.1, s32[1,4,8]{2,1,0:T(4,128)} %target_ids.1, s32[1,4,8]{2,1,0:T(4,128)} %class_ids.1, s32[1,4]{1,0:T(1,128)} %live_counts.1, s32[16,12]{1,0:T(8,128)} %partner_ids.1, bf16[16,16,128]{2,1,0:T(8,128)(2,1)} %hist_cur.1, ...), custom_call_target="tpu_custom_call" | custom-call | tf_op jit(solution)/shard_map/pallas_call | solution.py:384
  39.2 1.3 %copy.16 = bf16[16,4,128]{2,1,0:T(4,128)(2,1)} copy(bf16[16,4,128]{2,0,1:T(8,128)(2,1)} %bitcast.8) | data formatting | bytes 32768
  40.6 0.0 copy-done
  40.6 0.9 %convolution_convert_fusion = bf16[16,4,2560]{2,0,1:T(8,128)(2,1)S(1)} fusion(bf16[128,2560]{1,0:T(8,128)(2,1)S(1)} %copy-done, bf16[4,16,128]{2,1,0:T(8,128)(2,1)} %shard_map.149), kind=kOutput, calls=%fused_computation | convolution fusion | flops 42106880 | bytes 999424 | tf_op jit(solution)/shard_map/bts,sk->btk/dot_general | solution.py:437
  41.5 1.0 %copy.17 = bf16[16,4,2560]{2,1,0:T(4,128)(2,1)} copy(bf16[16,4,2560]{2,0,1:T(8,128)(2,1)S(1)} %convolution_convert_fusion) | data formatting | bytes 655360
Async XLA Ops:
  0.6 39.9 %copy-start = (bf16[128,2560]{1,0:T(8,128)(2,1)S(1)}, bf16[128,2560]{1,0:T(8,128)(2,1)}, u32[]{:S(2)}) copy-start(bf16[128,2560]{1,0:T(8,128)(2,1)} %projection_hbm.1) | copy-start | bytes 1966084

commit v4 on v3

--- a/solution.py
+++ b/solution.py
@@ -104,7 +104,9 @@
 
     barrier = pltpu.get_barrier_semaphore()
     for offset in range(1, peers):
-        pl.semaphore_signal(barrier, inc=1, device_id=peer_of(offset), device_id_type=MESH)
+        for turn_by in range(spread):
+            target = {**peer_of(offset), **sibling_of(turn_by)}
+            pl.semaphore_signal(barrier, inc=1, device_id=target, device_id_type=MESH)
     for offset in range(1, spread):
         pl.semaphore_signal(barrier, inc=1, device_id=sibling_of(offset), device_id_type=MESH)
 
@@ -145,7 +147,7 @@
     near_pick[...] = pick(partner - (box - 1) * boxes, 3 * boxes).astype(BF16)
     for copy in copies[3:]:
         copy.start()
-    pl.semaphore_wait(barrier, peers - 1 + spread - 1)
+    pl.semaphore_wait(barrier, peers * spread - 1)
 
     def window_copy(order, side):
         span = pl.ds(0, lag_span) if order == 0 else pl.ds(lag_span + order - 1, 1)
@@ -191,13 +193,13 @@
 
     start_window(0)
 
-    def far_copy(step, offset):
+    def far_copy(step, offset, turn_by):
         return pltpu.make_async_remote_copy(
             src_ref=far_send.at[step, lax.rem(box + offset, peers)],
-            dst_ref=far_recv.at[step, offset],
-            send_sem=far_send_sem.at[step, offset],
-            recv_sem=far_recv_sem.at[step, offset],
-            device_id=peer_of(offset),
+            dst_ref=far_recv.at[step, offset, piece],
+            send_sem=far_send_sem.at[step, offset * spread + turn_by],
+            recv_sem=far_recv_sem.at[step, offset * spread + turn_by],
+            device_id={**peer_of(offset), **sibling_of(turn_by)},
             device_id_type=MESH,
         )
 
@@ -252,9 +254,10 @@
         far = jnp.dot(
             target_pick[...], jnp.concatenate([high, low], axis=0), preferred_element_type=F32
         )
-        far_send[step] = far.reshape(peers, boxes, width)
+        far_send[step] = far.astype(BF16).reshape(peers, boxes, width)
         for offset in range(1, peers):
-            far_copy(step, offset).start()
+            for turn_by in range(spread):
+                far_copy(step, offset, turn_by).start()
 
     row = lax.broadcasted_iota(jnp.int32, (boxes, width), 0)
 
@@ -297,11 +300,7 @@
         field = jnp.zeros((boxes, width), F32)
         for index in range(boxes):
             field = near_part(index, field)
-        field = field + far_send[step, box]
-        for offset in range(1, peers):
-            far_copy(step, offset).wait_recv()
-            field = field + far_recv[step, offset]
-        part[step, piece] = field
+        part[step, piece] = field + far_send[step, box].astype(F32)
         for offset in range(1, spread):
             part_copy(step, offset).start()
         if step == 0:
@@ -314,9 +313,16 @@
                 return carry
 
             lax.fori_loop(0, boxes, turn, 0)
+        for offset in range(1, peers):
+            for turn_by in range(spread):
+                far_copy(step, offset, turn_by).wait_recv()
+        around = jnp.zeros((boxes, width), F32)
+        for offset in range(1, peers):
+            for other in range(spread):
+                around = around + far_recv[step, offset, other].astype(F32)
         for offset in range(1, spread):
             part_copy(step, offset).wait_recv()
-        total = part[step, 0]
+        total = around + part[step, 0]
         for other in range(1, spread):
             total = total + part[step, other]
 
@@ -348,7 +354,8 @@
     for step in range(steps):
         wait_window_sent(step)
         for offset in range(1, peers):
-            far_copy(step, offset).wait_send()
+            for turn_by in range(spread):
+                far_copy(step, offset, turn_by).wait_send()
         for offset in range(1, spread):
             part_copy(step, offset).wait_send()
 
@@ -403,14 +410,14 @@
             pltpu.VMEM((peers * boxes, 2 * slots), BF16),
             pltpu.VMEM((slots, rays), BF16),
             pltpu.VMEM((steps * slots, width), F32),
-            pltpu.VMEM((steps, peers, boxes, width), F32),
-            pltpu.VMEM((steps, peers, boxes, width), F32),
+            pltpu.VMEM((steps, peers, boxes, width), BF16),
+            pltpu.VMEM((steps, peers, spread, boxes, width), BF16),
             pltpu.VMEM((steps, spread, boxes, width), F32),
             dma((6,)),
             dma((steps, 2)),
             dma((steps, 2)),
-            dma((steps, peers)),
-            dma((steps, peers)),
+            dma((steps, peers * spread)),
+            dma((steps, peers * spread)),
             dma((steps, spread)),
             dma((steps, spread)),
         ],

time: 42.8 us -> 41.2 us (0.963)
  Pallas kernels: 38.6 us -> 37 us
    pallas_call x1, Pallas kernels: 38.6 us -> 37 us  [body(): pl.pallas_call(functools.partial(march, peers, dirs, subs), out_shape=jax...]
where the time goes in v4:
time: 41.2 us; the launch traced here: 40.9 us
  Pallas kernels  37 us (90%)
  local copies, waits for them, and re-layouts  2.31 us (6%)
  matrix products  0.95 us (2%)
  between operations  0.66 us (2%)
    pallas_call x1, Pallas kernels, body(): pl.pallas_call(functools.partial(march, peers, dirs, subs), out_shape=jax...  37 us
    unnamed x4, local copies, waits for them, and re-layouts  2.31 us
    dot_general x1, matrix products, body(): jnp.einsum('bts,sk->btk', currents, projection, preferred_element_type=F32)  0.95 us

profile of v4, /device:TPU:0, one launch (start us, length us, event | category | flops | bytes accessed | tf_op | source)
XLA Modules:
  0.0 40.9 jit_solution(13108630059442527926)
XLA Ops:
  0.6 0.0 copy-start
  0.6 37.0 %shard_map.149 = bf16[4,16,128]{2,1,0:T(8,128)(2,1)} custom-call(s32[1,4,8]{2,1,0:T(4,128)} %source_ids.1, s32[1,4,8]{2,1,0:T(4,128)} %delay_ids.1, s32[1,4,8]{2,1,0:T(4,128)} %target_ids.1, s32[1,4,8]{2,1,0:T(4,128)} %class_ids.1, s32[1,4]{1,0:T(1,128)} %live_counts.1, s32[16,12]{1,0:T(8,128)} %partner_ids.1, bf16[16,16,128]{2,1,0:T(8,128)(2,1)} %hist_cur.1, ...), custom_call_target="tpu_custom_call" | custom-call | tf_op jit(solution)/shard_map/pallas_call | solution.py:391
  37.6 1.3 %copy.16 = bf16[16,4,128]{2,1,0:T(4,128)(2,1)} copy(bf16[16,4,128]{2,0,1:T(8,128)(2,1)} %bitcast.8) | data formatting | bytes 32768
  39.0 0.0 copy-done
  39.0 0.9 %convolution_convert_fusion = bf16[16,4,2560]{2,0,1:T(8,128)(2,1)S(1)} fusion(bf16[128,2560]{1,0:T(8,128)(2,1)S(1)} %copy-done, bf16[4,16,128]{2,1,0:T(8,128)(2,1)} %shard_map.149), kind=kOutput, calls=%fused_computation | convolution fusion | flops 42106880 | bytes 999424 | tf_op jit(solution)/shard_map/bts,sk->btk/dot_general | solution.py:444
  39.9 1.0 %copy.17 = bf16[16,4,2560]{2,1,0:T(4,128)(2,1)} copy(bf16[16,4,2560]{2,0,1:T(8,128)(2,1)S(1)} %convolution_convert_fusion) | data formatting | bytes 655360
Async XLA Ops:
  0.6 38.3 %copy-start = (bf16[128,2560]{1,0:T(8,128)(2,1)S(1)}, bf16[128,2560]{1,0:T(8,128)(2,1)}, u32[]{:S(2)}) copy-start(bf16[128,2560]{1,0:T(8,128)(2,1)} %projection_hbm.1) | copy-start | bytes 1966084

commit v5 on v4

--- a/solution.py
+++ b/solution.py
@@ -345,7 +345,7 @@
         for index in range(boxes):
             current = solve_part(index, current)
         current = current.astype(BF16)
-        out[step] = current
+        out[:, pl.ds(step * width, width)] = current
         if step < steps - 1:
             cur_all[pl.ds(step * boxes, boxes), :] = current
             win[1, lag_span + step] = current.astype(F32)
@@ -390,7 +390,7 @@
     dma = pltpu.SemaphoreType.DMA
     currents = pl.pallas_call(
         functools.partial(march, peers, dirs, subs),
-        out_shape=jax.ShapeDtypeStruct((steps, boxes, width), BF16),
+        out_shape=jax.ShapeDtypeStruct((boxes, steps * width), BF16),
         in_specs=[smem] * 6 + [vmem] * 2 + [hbm] * 6,
         out_specs=vmem,
         scratch_shapes=[
@@ -440,7 +440,7 @@
         reception,
         translations,
     )
-    currents = currents.transpose(1, 0, 2)
+    currents = currents.reshape(boxes, steps, width)
     new_rays = jnp.einsum("bts,sk->btk", currents, projection, preferred_element_type=F32)
     return currents, new_rays.astype(BF16)
 

time: 41.2 us -> 41.2 us (level)
    reshape x0 -> x1, local copies, waits for them, and re-layouts: none -> 1.33 us  [body(): currents = currents.reshape(boxes, steps, width)]
    unnamed x4 -> x3, local copies, waits for them, and re-layouts: 2.31 us -> 0.98 us
where the time goes in v5:
time: 41.2 us; the launch traced here: 40.9 us
  Pallas kernels  37 us (90%)
  local copies, waits for them, and re-layouts  2.32 us (6%)
  matrix products  0.95 us (2%)
  between operations  0.66 us (2%)
    pallas_call x1, Pallas kernels, body(): pl.pallas_call(functools.partial(march, peers, dirs, subs), out_shape=jax...  37 us
    reshape x1, local copies, waits for them, and re-layouts, body(): currents = currents.reshape(boxes, steps, width)  1.33 us
    unnamed x3, local copies, waits for them, and re-layouts  0.98 us
    dot_general x1, matrix products, body(): jnp.einsum('bts,sk->btk', currents, projection, preferred_element_type=F32)  0.95 us

profile of v5, /device:TPU:0, one launch (start us, length us, event | category | flops | bytes accessed | tf_op | source)
XLA Modules:
  0.0 40.9 jit_solution(16505415716317196424)
XLA Ops:
  0.6 0.0 copy-start
  0.6 37.0 %shard_map.149 = bf16[16,512]{1,0:T(8,128)(2,1)} custom-call(s32[1,4,8]{2,1,0:T(4,128)} %source_ids.1, s32[1,4,8]{2,1,0:T(4,128)} %delay_ids.1, s32[1,4,8]{2,1,0:T(4,128)} %target_ids.1, s32[1,4,8]{2,1,0:T(4,128)} %class_ids.1, s32[1,4]{1,0:T(1,128)} %live_counts.1, s32[16,12]{1,0:T(8,128)} %partner_ids.1, bf16[16,16,128]{2,1,0:T(8,128)(2,1)} %hist_cur.1, ...), custom_call_target="tpu_custom_call" | custom-call | tf_op jit(solution)/shard_map/pallas_call | solution.py:391
  37.6 1.3 %reshape.11 = bf16[16,4,128]{2,1,0:T(4,128)(2,1)} reshape(bf16[16,512]{1,0:T(8,128)(2,1)} %shard_map.149) | data formatting | bytes 32768 | tf_op jit(solution)/shard_map/reshape | solution.py:443
  39.0 0.0 copy-done
  39.0 0.9 %convolution_convert_fusion = bf16[16,4,2560]{2,0,1:T(8,128)(2,1)S(1)} fusion(bf16[128,2560]{1,0:T(8,128)(2,1)S(1)} %copy-done, bf16[16,512]{1,0:T(8,128)(2,1)} %shard_map.149), kind=kOutput, calls=%fused_computation | convolution fusion | flops 42106880 | bytes 999424 | tf_op jit(solution)/shard_map/bts,sk->btk/dot_general | solution.py:444
  39.9 1.0 %copy.17 = bf16[16,4,2560]{2,1,0:T(4,128)(2,1)} copy(bf16[16,4,2560]{2,0,1:T(8,128)(2,1)S(1)} %convolution_convert_fusion) | data formatting | bytes 655360
Async XLA Ops:
  0.6 38.3 %copy-start = (bf16[128,2560]{1,0:T(8,128)(2,1)S(1)}, bf16[128,2560]{1,0:T(8,128)(2,1)}, u32[]{:S(2)}) copy-start(bf16[128,2560]{1,0:T(8,128)(2,1)} %projection_hbm.1) | copy-start | bytes 1966084
